TPU v7x, 1024 devices: a whole 4x8x16 slice. The times are simulated.
1024 devices in a mesh: wide: 64 (over y, x, core), narrow: 16 (over z).
Axes of the slice: x: 4, y: 8, z: 16, core: 2. Of those that a mesh axis runs over, the one named last changes fastest.
Arguments:
- tokens: bfloat16 [4096, 4096], P('wide', 'narrow'), may hold values from -6 to 6
- cotangent: bfloat16 [4096, 4096], P('wide', 'narrow'), may hold values from -6 to 6
- expert_ids: int32 [4096, 1], P('wide'), may hold values from 0 to 63; in each aligned block of 64 rows (0 to 63, 64 to 127, ...) at most 2 rows name the same one
- gate_weight: bfloat16 [64, 4096, 2048], P('wide', None, 'narrow'), may hold values from -0.125 to 0.125
- up_weight: bfloat16 [64, 4096, 2048], P('wide', None, 'narrow'), may hold values from -0.125 to 0.125
- down_weight: bfloat16 [64, 2048, 4096], P('wide', 'narrow'), may hold values from -0.1875 to 0.1875
Outputs:
- mixed: bfloat16 [4096, 4096], P('wide', 'narrow')
- grad_tokens: bfloat16 [4096, 4096], P('wide', 'narrow')
Inputs may be any that keep to these rules, and one draw needn't show every extreme that they name: `expert_ids`: within each group of 64 consecutive tokens no expert is named by more than 2 tokens, and in some group an expert is named by exactly 2. Every expert is named by some token.
All inputs are finite; a program needn't handle non-finite values.
Results may differ from a plain program's by a relative error of at most 0.024.
Values may be sent and summed in bfloat16 or wider, within the bound.
A program may use at most 32 MiB of HBM per device.

v0:
```python
import jax
import jax.numpy as jnp
from jax import lax
from jax.sharding import PartitionSpec as P

CAP = 2


def per_device(tokens, cotangent, expert_ids, gate_weight, up_weight, down_weight):
    groups = lax.axis_size("wide")
    slots = groups * CAP
    ids = expert_ids[:, 0]
    onehot = (ids[:, None] == jnp.arange(groups, dtype=jnp.int32)[None, :]).astype(jnp.int32)
    before = jnp.cumsum(onehot, axis=0) - onehot
    target = ids * CAP + jnp.sum(before * onehot, axis=1)
    placing = (jnp.arange(slots, dtype=jnp.int32)[:, None] == target[None, :]).astype(jnp.bfloat16)

    def dispatch(rows):
        spread = jnp.dot(placing, rows, preferred_element_type=jnp.float32).astype(jnp.bfloat16)
        return spread.reshape(groups, CAP, rows.shape[1])

    whole_tok, whole_cot = (
        lax.all_gather(tokens, "narrow", axis=1, tiled=True),
        lax.all_gather(cotangent, "narrow", axis=1, tiled=True),
    )
    sent_tok = lax.all_to_all(dispatch(whole_tok), "wide", split_axis=0, concat_axis=0, tiled=True)
    sent_cot = lax.all_to_all(dispatch(whole_cot), "wide", split_axis=0, concat_axis=0, tiled=True)
    rows_in = sent_tok.reshape(slots, sent_tok.shape[2])
    cots_in = sent_cot.reshape(slots, sent_cot.shape[2])
    w_gate = gate_weight[0]
    w_up = up_weight[0]
    w_down = down_weight[0]
    gate = jnp.dot(rows_in, w_gate, preferred_element_type=jnp.float32)
    up = jnp.dot(rows_in, w_up, preferred_element_type=jnp.float32)
    sig = jax.nn.sigmoid(gate)
    hidden = (gate * sig * up).astype(jnp.bfloat16)
    out_term = jnp.dot(hidden, w_down, preferred_element_type=jnp.float32)
    contract = (((1,), (1,)), ((), ()))
    back = lax.dot_general(cots_in, w_down, contract, preferred_element_type=jnp.float32)
    d_gate = (back * up * sig * (1.0 + gate * (1.0 - sig))).astype(jnp.bfloat16)
    d_up = (back * gate * sig).astype(jnp.bfloat16)
    in_term = lax.dot_general(d_gate, w_gate, contract, preferred_element_type=jnp.float32)
    in_term = in_term + lax.dot_general(d_up, w_up, contract, preferred_element_type=jnp.float32)
    out_part, in_part = (
        lax.psum_scatter(
            out_term.astype(jnp.bfloat16), "narrow", scatter_dimension=1, tiled=True
        ).astype(jnp.float32),
        lax.psum_scatter(
            in_term.astype(jnp.bfloat16), "narrow", scatter_dimension=1, tiled=True
        ).astype(jnp.float32),
    )
    width = out_part.shape[1]
    out_rows = out_part.astype(jnp.bfloat16).reshape(groups, CAP, width)
    in_rows = in_part.astype(jnp.bfloat16).reshape(groups, CAP, width)
    back_out, back_in = (
        lax.all_to_all(out_rows, "wide", split_axis=0, concat_axis=0, tiled=True),
        lax.all_to_all(in_rows, "wide", split_axis=0, concat_axis=0, tiled=True),
    )
    gather_dims = (((0,), (0,)), ((), ()))
    mixed = lax.dot_general(
        placing, back_out.reshape(slots, width), gather_dims, preferred_element_type=jnp.float32
    )
    grad_tokens = lax.dot_general(
        placing, back_in.reshape(slots, width), gather_dims, preferred_element_type=jnp.float32
    )
    return (mixed.astype(jnp.bfloat16), grad_tokens.astype(jnp.bfloat16))


def solution(mesh):
    placed = (
        P("wide", "narrow"),
        P("wide", "narrow"),
        P("wide", None),
        P("wide", None, "narrow"),
        P("wide", None, "narrow"),
        P("wide", "narrow", None),
    )
    return jax.shard_map(
        per_device,
        mesh=mesh,
        in_specs=placed,
        out_specs=(P("wide", "narrow"), P("wide", "narrow")),
        check_vma=False,
    )
```

profile of v0, /device:TPU:1, one launch (start us, length us, event | category | flops | bytes accessed | tf_op | source)
XLA Modules:
  0.0 287.7 jit_solution(16845857012825516324)
XLA Ops:
  7.2 0.8 fusion.18
  8.1 0.8 select_reduce_fusion
  8.9 0.7 multiply_add_fusion
  9.6 39.5 %all_gather.6 = bf16[64,4096]{1,0:T(8,128)(2,1)S(1)} all-gather(bf16[64,256]{1,0:T(8,128)(2,1)} %param.6), channel_id=1, replica_groups=mesh['wide'=64,'narrow'=16] {'narrow'}, dimensions={1}, use_global_device_ids=true | all-gather | bytes 557056 | tf_op jit(solution)/shard_map/all_gather | solution.py:23
  49.1 0.4 convolution_convert_fusion.2
  49.5 1.5 reshape.36
  51.0 17.4 %all-to-all-start = ((bf16[64,2,4096]{2,1,0:T(2,128)(2,1)}), bf16[64,2,4096]{2,1,0:T(2,128)(2,1)S(1)}, u32[]{:S(2)}, u32[]{:S(2)}) async-start(bf16[64,2,4096]{2,1,0:T(2,128)(2,1)} %reshape.36), calls=%async_computation | async-start | bytes 2097152 | tf_op jit(solution)/shard_map/all_to_all | solution.py:26
  68.4 24.4 %all_gather.7 = bf16[64,4096]{1,0:T(8,128)(2,1)S(1)} all-gather(bf16[64,256]{1,0:T(8,128)(2,1)S(1)} %copy-done.5), channel_id=1, replica_groups=mesh['wide'=64,'narrow'=16] {'narrow'}, dimensions={1}, use_global_device_ids=true | all-gather | bytes 557056 | tf_op jit(solution)/shard_map/all_gather | solution.py:24
  92.8 0.4 convolution_convert_fusion
  93.2 1.5 reshape.40
  94.7 1.7 all-to-all-done
  96.4 13.3 %all-to-all-start.2 = ((bf16[64,2,4096]{2,1,0:T(2,128)(2,1)}), bf16[64,2,4096]{2,1,0:T(2,128)(2,1)}, u32[]{:S(2)}, u32[]{:S(2)}) async-start(bf16[64,2,4096]{2,1,0:T(2,128)(2,1)} %reshape.40), calls=%async_computation.3 | async-start | bytes 2097152 | tf_op jit(solution)/shard_map/all_to_all | solution.py:27
  109.8 1.5 reshape.37
  111.3 0.4 fusion.9
  111.7 0.8 copy-done.3
  112.5 0.4 fusion.5
  112.9 1.5 convolution_convert_fusion.1
  114.5 23.1 %all-to-all-done.2 = bf16[64,2,4096]{2,1,0:T(2,128)(2,1)} async-done(((bf16[64,2,4096]{2,1,0:T(2,128)(2,1)}), bf16[64,2,4096]{2,1,0:T(2,128)(2,1)}, u32[]{:S(2)}, u32[]{:S(2)}) %all-to-all-start.2) | async-done | bytes 1048608 | tf_op jit(solution)/shard_map/all_to_all | solution.py:27
  137.6 1.5 reshape.41
  139.1 0.4 fusion.1
  139.5 0.4 fusion.7
  140.0 0.8 copy-done.4
  140.8 1.4 fusion
  142.2 30.3 %reduce-scatter.3.cloned.1.call-done = bf16[128,256]{1,0:T(8,128)(2,1)} async-done(((bf16[128,4096]{1,0:T(8,128)(2,1)}), bf16[128,256]{1,0:T(8,128)(2,1)}) %reduce-scatter.3.cloned.1.call-update) | async-done | bytes 65552 | tf_op jit(solution)/shard_map/reduce_scatter | solution.py:45
  172.5 1.5 reshape.38
  174.0 20.5 %all-to-all-start.1 = ((bf16[64,2,256]{2,1,0:T(2,128)(2,1)}), bf16[64,2,256]{2,1,0:T(2,128)(2,1)S(1)}, u32[]{:S(2)}, u32[]{:S(2)}) async-start(bf16[64,2,256]{2,1,0:T(2,128)(2,1)} %reshape.38), calls=%async_computation.2 | async-start | bytes 131072 | tf_op jit(solution)/shard_map/all_to_all | solution.py:56
  194.5 52.8 %reduce-scatter.5.cloned.1.call-done = bf16[128,256]{1,0:T(8,128)(2,1)} async-done(((bf16[128,4096]{1,0:T(8,128)(2,1)}), bf16[128,256]{1,0:T(8,128)(2,1)}) %reduce-scatter.5.cloned.1.call-update) | async-done | bytes 65552 | tf_op jit(solution)/shard_map/reduce_scatter | solution.py:48
  247.3 1.5 reshape.42
  248.8 21.1 %all-to-all-start.3 = ((bf16[64,2,256]{2,1,0:T(2,128)(2,1)}), bf16[64,2,256]{2,1,0:T(2,128)(2,1)S(1)}, u32[]{:S(2)}, u32[]{:S(2)}) async-start(bf16[64,2,256]{2,1,0:T(2,128)(2,1)} %reshape.42), calls=%async_computation.5 | async-start | bytes 131072 | tf_op jit(solution)/shard_map/all_to_all | solution.py:57
  270.0 0.8 convolution_convert_fusion.4
  270.8 9.2 %all-to-all-done.3 = bf16[64,2,256]{2,1,0:T(2,128)(2,1)S(1)} async-done(((bf16[64,2,256]{2,1,0:T(2,128)(2,1)}), bf16[64,2,256]{2,1,0:T(2,128)(2,1)S(1)}, u32[]{:S(2)}, u32[]{:S(2)}) %all-to-all-start.3) | async-done | bytes 65568 | tf_op jit(solution)/shard_map/all_to_all | solution.py:57
  280.1 0.8 convolution_convert_fusion.3
  (18 shorter events, 0.3 us)
Async XLA Ops:
  7.2 105.8 %copy-start = (bf16[1,128,4096]{2,1,0:T(8,128)(2,1)S(1)}, bf16[1,128,4096]{2,1,0:T(8,128)(2,1)}, u32[]{:S(2)}) copy-start(bf16[1,128,4096]{2,1,0:T(8,128)(2,1)} %param.11) | copy-start | bytes 3145732
  49.5 18.9 %copy-start.5 = (bf16[64,256]{1,0:T(8,128)(2,1)S(1)}, bf16[64,256]{1,0:T(8,128)(2,1)}, u32[]{:S(2)}) copy-start(bf16[64,256]{1,0:T(8,128)(2,1)} %param.7) | copy-start | bytes 98308
  51.0 45.4 %all-to-all-start = ((bf16[64,2,4096]{2,1,0:T(2,128)(2,1)}), bf16[64,2,4096]{2,1,0:T(2,128)(2,1)S(1)}, u32[]{:S(2)}, u32[]{:S(2)}) async-start(bf16[64,2,4096]{2,1,0:T(2,128)(2,1)} %reshape.36), calls=%async_computation | async-start | bytes 2097152 | tf_op jit(solution)/shard_map/all_to_all | solution.py:26
  94.7 16.5 %copy-start.1 = (bf16[1,4096,128]{2,1,0:T(8,128)(2,1)S(1)}, bf16[1,4096,128]{2,1,0:T(8,128)(2,1)}, u32[]{:S(2)}) copy-start(bf16[1,4096,128]{2,1,0:T(8,128)(2,1)} %param.9) | copy-start | bytes 3145732
  96.4 13.3 %copy-start.2 = (bf16[64,2,4096]{2,1,0:T(2,128)(2,1)}, bf16[64,2,4096]{2,1,0:T(2,128)(2,1)S(1)}, u32[]{:S(2)}) copy-start(bf16[64,2,4096]{2,1,0:T(2,128)(2,1)S(1)} %all-to-all-done) | copy-start | bytes 3145732
  96.4 41.2 %all-to-all-start.2 = ((bf16[64,2,4096]{2,1,0:T(2,128)(2,1)}), bf16[64,2,4096]{2,1,0:T(2,128)(2,1)}, u32[]{:S(2)}, u32[]{:S(2)}) async-start(bf16[64,2,4096]{2,1,0:T(2,128)(2,1)} %reshape.40), calls=%async_computation.3 | async-start | bytes 2097152 | tf_op jit(solution)/shard_map/all_to_all | solution.py:27
  109.7 62.8 %reduce-scatter.3.cloned.1.call-start = ((), (), s32[]{:S(2)}) async-start(), calls=%async_computation.6 | async-start | bytes 1114112 | tf_op jit(solution)/shard_map/reduce_scatter | solution.py:45
  111.3 1.2 copy-start.3
  114.4 132.9 %reduce-scatter.5.cloned.1.call-start = ((), (), s32[]{:S(2)}) async-start(), calls=%async_computation.7 | async-start | bytes 1114112 | tf_op jit(solution)/shard_map/reduce_scatter | solution.py:48
  139.5 1.2 copy-start.4
  174.0 74.8 %all-to-all-start.1 = ((bf16[64,2,256]{2,1,0:T(2,128)(2,1)}), bf16[64,2,256]{2,1,0:T(2,128)(2,1)S(1)}, u32[]{:S(2)}, u32[]{:S(2)}) async-start(bf16[64,2,256]{2,1,0:T(2,128)(2,1)} %reshape.38), calls=%async_computation.2 | async-start | bytes 131072 | tf_op jit(solution)/shard_map/all_to_all | solution.py:56
  248.8 31.2 %all-to-all-start.3 = ((bf16[64,2,256]{2,1,0:T(2,128)(2,1)}), bf16[64,2,256]{2,1,0:T(2,128)(2,1)S(1)}, u32[]{:S(2)}, u32[]{:S(2)}) async-start(bf16[64,2,256]{2,1,0:T(2,128)(2,1)} %reshape.42), calls=%async_computation.5 | async-start | bytes 131072 | tf_op jit(solution)/shard_map/all_to_all | solution.py:57
Sparse Core Ops, SparseCore 0:
  114.5 57.9 reduce-scatter.2
  176.3 70.9 reduce-scatter.4
where the time goes:
time: 288 us
  waiting for transfers between devices  117 us (41%)
  starting transfers between devices  72.4 us (25%)
  blocking collectives  63.8 us (22%)
  between operations  14.2 us (5%)
  local copies, waits for them, and re-layouts  10.6 us (4%)
  matrix products  7.08 us (2%)
    reduce_scatter x1, waiting for transfers between devices, per_device(): lax.psum_scatter(in_term.astype(jnp.bfloat16), 'narrow', scatter_dimensio...  52.8 us
    all_gather x1, blocking collectives, per_device(): lax.all_gather(tokens, 'narrow', axis=1, tiled=True)  39.5 us
    reduce_scatter x1, waiting for transfers between devices, per_device(): lax.psum_scatter(out_term.astype(jnp.bfloat16), 'narrow', scatter_dimensi...  30.3 us
    all_gather x1, blocking collectives, per_device(): lax.all_gather(cotangent, 'narrow', axis=1, tiled=True)  24.4 us
    all_to_all x1, waiting for transfers between devices, per_device(): lax.all_to_all(dispatch(whole_cot), 'wide', split_axis=0, concat_axis=0,...  23.1 us
    all_to_all x1, starting transfers between devices, per_device(): lax.all_to_all(in_rows, 'wide', split_axis=0, concat_axis=0, tiled=True)  21.1 us
    all_to_all x1, starting transfers between devices, per_device(): lax.all_to_all(out_rows, 'wide', split_axis=0, concat_axis=0, tiled=True)  20.5 us
    all_to_all x1, starting transfers between devices, per_device(): lax.all_to_all(dispatch(whole_tok), 'wide', split_axis=0, concat_axis=0,...  17.4 us
  transfers between devices with their start and end apart: 6, of which 5 were waited for; matrix products, arithmetic and copies ran while one was open for 5% of the time, Pallas kernels for 0%

commit v1 on v0

v1 whole, which is shorter than its diff:
```python
import functools

import jax
import jax.numpy as jnp
from jax import lax
from jax.experimental import pallas as pl
from jax.experimental.pallas import tpu as pltpu
from jax.sharding import PartitionSpec as P

CAP = 2
INNER = 8
CHUNKS = 2
MESH = pl.DeviceIdType.MESH
F32 = jnp.float32
BF16 = jnp.bfloat16
NT = (((1,), (1,)), ((), ()))


def log2(value):
    return value.bit_length() - 1


def kernel(
    outer, inner, ring, chunks,
    ids_ref, tok_ref, cot_ref, gate_ref, up_ref, down_ref, mixed_ref, gtok_ref,
    ids_v, raw, gu, dn, st1, rx1, st2, gat, gu_acc, back_acc, hid, dgu,
    sbuf, rbuf, bk1, bx1, bk2, bx2, outv,
    in_sem, w_sem, out_sem, a_send, a_recv, g_send, g_recv, r_send, r_recv,
):
    slots = outer * inner * CAP
    group, width = raw.shape[1:]
    ff = hid.shape[1]
    part = slots // chunks
    wide = lax.axis_index("wide")
    me = lax.axis_index("narrow")
    my_o = wide // inner
    my_i = lax.rem(wide, inner)
    right = (wide, lax.rem(me + 1, ring))
    left = (wide, lax.rem(me + ring - 1, ring))

    first = [
        pltpu.make_async_copy(ids_ref, ids_v, in_sem.at[0]),
        pltpu.make_async_copy(tok_ref, raw.at[0], in_sem.at[1]),
        pltpu.make_async_copy(cot_ref, raw.at[1], in_sem.at[2]),
    ]
    weights = [
        pltpu.make_async_copy(gate_ref.at[0], gu.at[:, pl.ds(0, ff)], w_sem.at[0]),
        pltpu.make_async_copy(up_ref.at[0], gu.at[:, pl.ds(ff, ff)], w_sem.at[1]),
        pltpu.make_async_copy(down_ref.at[0], dn, w_sem.at[2]),
    ]
    for copy in first + weights:
        copy.start()

    outer_peers = [lax.rem(my_o + k, outer) for k in range(1, outer)]
    inner_peers = [lax.rem(my_i + k, inner) for k in range(1, inner)]
    peers = [(o * inner + my_i, me) for o in outer_peers]
    peers += [(my_o * inner + i, me) for i in inner_peers]
    peers += [right, left]
    barrier = pltpu.get_barrier_semaphore()
    for peer in peers:
        pl.semaphore_signal(barrier, inc=1, device_id=peer, device_id_type=MESH)

    for copy in first:
        copy.wait()
    ids_row = jnp.broadcast_to(ids_v[...].astype(F32), (group, group))
    i0 = lax.broadcasted_iota(jnp.int32, (group, group), 0)
    i1 = lax.broadcasted_iota(jnp.int32, (group, group), 1)
    ids_col = jnp.sum(jnp.where(i0 == i1, ids_row, 0.0), axis=1, keepdims=True)
    same = ids_col == ids_row
    slot_row = jnp.sum(jnp.where(same & (i0 < i1), 1.0, 0.0), axis=0, keepdims=True)
    slot_col = jnp.sum(jnp.where(same & (i1 < i0), 1.0, 0.0), axis=1, keepdims=True)
    target_row = (ids_row[:1] * CAP + slot_row).astype(jnp.int32)
    target_col = (ids_col * CAP + slot_col).astype(jnp.int32)
    spread = (lax.broadcasted_iota(jnp.int32, (slots, group), 0) == target_row).astype(BF16)
    collect = (lax.broadcasted_iota(jnp.int32, (group, slots), 1) == target_col).astype(BF16)
    r0 = lax.broadcasted_iota(jnp.int32, (slots, slots), 0)
    r1 = lax.broadcasted_iota(jnp.int32, (slots, slots), 1)

    def turned(r, low, high):
        cap, a, b = r & (CAP - 1), (r >> 1) & (low - 1), r >> (1 + log2(low))
        return (a * high + b) * CAP + cap

    to_inner = (r1 == turned(r0, outer, inner)).astype(BF16)
    to_outer = (r1 == turned(r0, inner, outer)).astype(BF16)

    pl.semaphore_wait(barrier, len(peers))

    def rows_of(index, count):
        return pl.ds(pl.multiple_of(index * count, count), count)

    def swap(stage, t, src, dst, to_outer_peers):
        count = inner * CAP if to_outer_peers else outer * CAP
        mine = my_o if to_outer_peers else my_i
        targets = outer_peers if to_outer_peers else inner_peers
        for k, p in enumerate(targets):
            device = (p * inner + my_i, me) if to_outer_peers else (my_o * inner + p, me)
            pltpu.make_async_remote_copy(
                src_ref=src.at[rows_of(p, count)],
                dst_ref=dst.at[rows_of(mine, count)],
                send_sem=a_send.at[stage, t],
                recv_sem=a_recv.at[stage, t],
                device_id=device,
                device_id_type=MESH,
            ).start()
        dst[rows_of(mine, count)] = src[rows_of(mine, count)]

    def swap_wait(stage, t, src, dst, to_outer_peers, send):
        count = inner * CAP if to_outer_peers else outer * CAP
        moved = pl.ds(0, slots - count)
        sem = a_send if send else a_recv
        pltpu.make_async_copy(src.at[moved], dst.at[moved], sem.at[stage, t]).wait()

    for t in range(2):
        st1[t] = jnp.dot(spread, raw[t], preferred_element_type=F32).astype(BF16)
        swap(0, t, st1.at[t], rx1.at[t], True)
    for t in range(2):
        swap_wait(0, t, st1.at[t], rx1.at[t], True, False)
        st2[t] = jnp.dot(to_inner, rx1[t], preferred_element_type=F32).astype(BF16)
        swap(1, t, st2.at[t], gat.at[t, me], False)

    def hops(t, d):
        longer = ring // 2
        return longer if t == d else ring - 1 - longer

    def gather_copy(t, d, s, c):
        owner = lax.rem(me + (ring - s if d == 0 else s), ring)
        chunk = gat.at[t, owner, pl.ds(c * part, part)]
        return pltpu.make_async_remote_copy(
            src_ref=chunk, dst_ref=chunk,
            send_sem=g_send.at[t, d, s], recv_sem=g_recv.at[t, d, s, c],
            device_id=right if d == 0 else left, device_id_type=MESH,
        )

    def gather_send(t, d, s):
        for c in range(chunks):
            gather_copy(t, d, s, c).start()

    def gather_sent(t, d, s):
        block = gat.at[t, 0]
        pltpu.make_async_copy(block, block, g_send.at[t, d, s]).wait()

    def use_block(t, owner):
        block = gat[t, owner]
        if t == 0:
            gu_acc[...] += jnp.dot(block, gu[rows_of(owner, width)], preferred_element_type=F32)
        else:
            back_acc[...] += lax.dot_general(
                block, dn[:, rows_of(owner, width)], NT, preferred_element_type=F32
            )

    def gather_step(t, s):
        for c in range(chunks):
            for d in range(2):
                if s < hops(t, d):
                    gather_copy(t, d, s, c).wait_recv()
                    if s + 1 < hops(t, d):
                        gather_copy(t, d, s + 1, c).start()
        for d in range(2):
            if s < hops(t, d):
                use_block(t, lax.rem(me + (ring - 1 - s if d == 0 else 1 + s), ring))
                gather_sent(t, d, s)

    def term(u, dest):
        if u == 0:
            return jnp.dot(hid[...], dn[:, rows_of(dest, width)], preferred_element_type=F32)
        return lax.dot_general(dgu[...], gu[rows_of(dest, width)], NT, preferred_element_type=F32)

    def sum_copy(u, d, s, c):
        chunk = pl.ds(c * part, part)
        return pltpu.make_async_remote_copy(
            src_ref=sbuf.at[u, d, s, chunk], dst_ref=rbuf.at[u, d, s, chunk],
            send_sem=r_send.at[u, d, s], recv_sem=r_recv.at[u, d, s, c],
            device_id=right if d == 0 else left, device_id_type=MESH,
        )

    def sum_step(u, s):
        live = [d for d in range(2) if s < hops(u, d)]
        terms = {}
        for d in live:
            far = hops(u, d) - s
            terms[d] = term(u, lax.rem(me + (far if d == 0 else ring - far), ring))
        for c in range(chunks):
            chunk = pl.ds(c * part, part)
            for d in live:
                value = terms[d][c * part:(c + 1) * part]
                if s > 0:
                    sum_copy(u, d, s - 1, c).wait_recv()
                    value = value + rbuf[u, d, s - 1, chunk].astype(F32)
                sbuf[u, d, s, chunk] = value.astype(BF16)
                sum_copy(u, d, s, c).start()

    def sum_end(u):
        total = term(u, me)
        for c in range(chunks):
            chunk = pl.ds(c * part, part)
            value = total[c * part:(c + 1) * part]
            for d in range(2):
                last = hops(u, d) - 1
                sum_copy(u, d, last, c).wait_recv()
                value = value + rbuf[u, d, last, chunk].astype(F32)
            bk1[u, chunk] = value.astype(BF16)
        swap(2, u, bk1.at[u], bx1.at[u], False)

    def back_turn(u):
        swap_wait(2, u, bk1.at[u], bx1.at[u], False, False)
        bk2[u] = jnp.dot(to_outer, bx1[u], preferred_element_type=F32).astype(BF16)
        swap(3, u, bk2.at[u], bx2.at[u], True)

    def back_end(u):
        swap_wait(3, u, bk2.at[u], bx2.at[u], True, False)
        outv[u] = jnp.dot(collect, bx2[u], preferred_element_type=F32).astype(BF16)
        pltpu.make_async_copy(outv.at[u], (mixed_ref, gtok_ref)[u], out_sem.at[u]).start()

    def sum_sent(u, d, s):
        pltpu.make_async_copy(sbuf.at[u, d, s], rbuf.at[u, d, s], r_send.at[u, d, s]).wait()

    gu_acc[...] = jnp.zeros_like(gu_acc)
    back_acc[...] = jnp.zeros_like(back_acc)
    for t in range(2):
        swap_wait(1, t, st2.at[t], gat.at[t, me], False, False)
        for d in range(2):
            gather_send(t, d, 0)
    for copy in weights:
        copy.wait()
    for t in range(2):
        use_block(t, me)
        swap_wait(0, t, st1.at[t], rx1.at[t], True, True)
        swap_wait(1, t, st2.at[t], gat.at[t, me], False, True)

    longest = ring // 2
    for s in range(longest):
        gather_step(0, s)
    gate = gu_acc[:, :ff]
    up = gu_acc[:, ff:]
    sig = jax.nn.sigmoid(gate)
    hid[...] = (gate * sig * up).astype(BF16)
    sum_step(0, 0)
    for s in range(longest):
        gather_step(1, s)
    gate = gu_acc[:, :ff]
    up = gu_acc[:, ff:]
    sig = jax.nn.sigmoid(gate)
    back = back_acc[...]
    dgu[:, :ff] = (back * up * sig * (1.0 + gate * (1.0 - sig))).astype(BF16)
    dgu[:, ff:] = (back * gate * sig).astype(BF16)
    sum_step(1, 0)
    for s in range(1, longest):
        sum_step(0, s)
    sum_end(0)
    for s in range(1, longest):
        sum_step(1, s)
        if s == longest // 3:
            back_turn(0)
        if s == 2 * longest // 3:
            back_end(0)
    sum_end(1)
    for u in range(2):
        for d in range(2):
            for s in range(hops(u, d)):
                sum_sent(u, d, s)
        swap_wait(2, 0, bk1.at[0], bx1.at[0], False, True) if u == 0 else None
    back_turn(1)
    swap_wait(3, 0, bk2.at[0], bx2.at[0], True, True)
    swap_wait(2, 1, bk1.at[1], bx1.at[1], False, True)
    back_end(1)
    swap_wait(3, 1, bk2.at[1], bx2.at[1], True, True)
    for u in range(2):
        pltpu.make_async_copy(outv.at[u], (mixed_ref, gtok_ref)[u], out_sem.at[u]).wait()


def per_device(inner, tokens, cotangent, expert_ids, gate_weight, up_weight, down_weight):
    groups, ring = lax.axis_size("wide"), lax.axis_size("narrow")
    outer = groups // inner
    slots = groups * CAP
    group, width = tokens.shape
    d_model, ff = gate_weight.shape[1:]
    longest = ring // 2
    out = jax.ShapeDtypeStruct((group, width), BF16)
    any_spec = pl.BlockSpec(memory_space=pl.ANY)
    block = (slots, width)
    dma = pltpu.SemaphoreType.DMA
    return pl.pallas_call(
        functools.partial(kernel, outer, inner, ring, CHUNKS),
        out_shape=(out, out),
        in_specs=[any_spec] * 6,
        out_specs=(any_spec, any_spec),
        scratch_shapes=[
            pltpu.VMEM((1, group), jnp.int32),
            pltpu.VMEM((2, group, width), BF16),
            pltpu.VMEM((d_model, 2 * ff), BF16),
            pltpu.VMEM((ff, d_model), BF16),
            pltpu.VMEM((2,) + block, BF16),
            pltpu.VMEM((2,) + block, BF16),
            pltpu.VMEM((2,) + block, BF16),
            pltpu.VMEM((2, ring) + block, BF16),
            pltpu.VMEM((slots, 2 * ff), F32),
            pltpu.VMEM((slots, ff), F32),
            pltpu.VMEM((slots, ff), BF16),
            pltpu.VMEM((slots, 2 * ff), BF16),
            pltpu.VMEM((2, 2, longest) + block, BF16),
            pltpu.VMEM((2, 2, longest) + block, BF16),
            pltpu.VMEM((2,) + block, BF16),
            pltpu.VMEM((2,) + block, BF16),
            pltpu.VMEM((2,) + block, BF16),
            pltpu.VMEM((2,) + block, BF16),
            pltpu.VMEM((2, group, width), BF16),
            dma((3,)),
            dma((3,)),
            dma((2,)),
            dma((4, 2)),
            dma((4, 2)),
            dma((2, 2, longest)),
            dma((2, 2, longest, CHUNKS)),
            dma((2, 2, longest)),
            dma((2, 2, longest, CHUNKS)),
        ],
        compiler_params=pltpu.CompilerParams(
            collective_id=0, has_side_effects=True, vmem_limit_bytes=40 * 1024 * 1024
        ),
        cost_estimate=pl.CostEstimate(
            flops=12 * slots * d_model * ff, bytes_accessed=6 * d_model * ff, transcendentals=slots * ff
        ),
    )(expert_ids.reshape(1, group), tokens, cotangent, gate_weight, up_weight, down_weight)


def solution(mesh):
    placed = (
        P("wide", "narrow"),
        P("wide", "narrow"),
        P("wide", None),
        P("wide", None, "narrow"),
        P("wide", None, "narrow"),
        P("wide", "narrow", None),
    )
    return jax.shard_map(
        functools.partial(per_device, INNER),
        mesh=mesh,
        in_specs=placed,
        out_specs=(P("wide", "narrow"), P("wide", "narrow")),
        check_vma=False,
    )
```

time: 288 us -> 151 us (0.52)
  Pallas kernels: 0 us -> 143 us
  waiting for transfers between devices: 117 us -> 0 us
  starting transfers between devices: 72.4 us -> 0 us
  blocking collectives: 63.8 us -> 0 us
  between operations: 14.2 us -> 0.65 us
  matrix products: 7.08 us -> 0 us
  local copies, waits for them, and re-layouts: 10.6 us -> 7.07 us
    pallas_call x0 -> x1, Pallas kernels: none -> 143 us  [per_device(): pl.pallas_call(functools.partial(kernel, outer, inner, ring, CHUNKS), out...]
    reduce_scatter x2 -> x0, waiting for transfers between devices: 83.1 us -> none  [the longest x1 52.8 us: per_device(): lax.psum_scatter(in_term.astype(jnp.bfloat16), 'narrow', scatter_dimensio...]
    all_to_all x4 -> x0, starting transfers between devices: 72.3 us -> none  [the longest x1 21.1 us: per_device(): lax.all_to_all(in_rows, 'wide', split_axis=0, concat_axis=0, tiled=True)]
    all_gather x2 -> x0, blocking collectives: 63.8 us -> none  [the longest x1 39.5 us: per_device(): lax.all_gather(tokens, 'narrow', axis=1, tiled=True)]
    all_to_all x4 -> x0, waiting for transfers between devices: 34.1 us -> none  [the longest x1 23.1 us: per_device(): lax.all_to_all(dispatch(whole_cot), 'wide', split_axis=0, concat_axis=0,...]
    reshape x8 -> x0, local copies, waits for them, and re-layouts: 9 us -> none  [the longest x2 3 us: dispatch(): return spread.reshape(groups, CAP, rows.shape[1])]
    dot_general x10 -> x0, matrix products: 7.08 us -> none  [the longest x1 1.46 us: per_device(): out_term = jnp.dot(hidden, w_down, preferred_element_type=jnp.float32)]
    unnamed x12 -> x14, local copies, waits for them, and re-layouts: 1.6 us -> 7.07 us
  transfers between devices with their start and end apart: 6 -> 0, of which waited for: 5 -> 0; matrix products, arithmetic and copies ran while one was open for 5% -> 0% of each run, Pallas kernels for 0% -> 0%
where the time goes in v1:
time: 151 us; the launch traced here: 150 us
  Pallas kernels  143 us (95%)
  local copies, waits for them, and re-layouts  7.07 us (5%)
    pallas_call x1, Pallas kernels, per_device(): pl.pallas_call(functools.partial(kernel, outer, inner, ring, CHUNKS), out...  143 us
    unnamed x14, local copies, waits for them, and re-layouts  7.07 us

profile of v1, /device:TPU:1, one launch (start us, length us, event | category | flops | bytes accessed | tf_op | source)
XLA Modules:
  0.0 150.3 jit_solution(5762396787298883393)
XLA Ops:
  0.6 0.0 copy-start.5
  0.6 0.6 copy-done.5
  1.3 0.0 copy-start
  1.3 1.2 copy-done
  2.5 0.0 copy-start.1
  2.5 1.2 copy-done.1
  3.7 0.0 copy-start.2
  3.7 1.2 copy-done.2
  5.0 0.0 copy-start.3
  5.0 0.8 copy-done.3
  5.7 0.0 copy-start.4
  5.7 0.8 copy-done.4
  6.5 142.6 %shard_map.77 = (bf16[64,256]{1,0:T(8,128)(2,1)S(1)}, bf16[64,256]{1,0:T(8,128)(2,1)S(1)}) custom-call(s32[1,64]{1,0:T(1,128)S(1)} %bitcast.1, bf16[64,256]{1,0:T(8,128)(2,1)S(1)} %copy-done.3, bf16[64,256]{1,0:T(8,128)(2,1)S(1)} %copy-done.4, bf16[1,4096,128]{2,1,0:T(8,128)(2,1)S(1)} %copy-done, bf16[1,4096,128]{2,1,0:T(8,128)(2,1)S(1)} %copy-done.1, ...), custom_call_target="tpu_custom_call" | custom-call | flops 805306368 | bytes 3145728 | tf_op jit(solution)/shard_map/pallas_call | solution.py:282
  149.1 0.6 copy.10
  149.7 0.6 copy.11
Async XLA Ops:
  0.6 0.7 copy-start.5
  1.3 1.2 copy-start
  2.5 1.2 copy-start.1
  3.7 1.2 copy-start.2
  5.0 0.8 copy-start.3
  5.7 0.8 copy-start.4

commit v2 on v1

--- a/solution.py
+++ b/solution.py
@@ -24,7 +24,7 @@
     outer, inner, ring, chunks,
     ids_ref, tok_ref, cot_ref, gate_ref, up_ref, down_ref, mixed_ref, gtok_ref,
     ids_v, raw, gu, dn, st1, rx1, st2, gat, gu_acc, back_acc, hid, dgu,
-    sbuf, rbuf, bk1, bx1, bk2, bx2, outv,
+    terms, sbuf, rbuf, bk1, bx1, bk2, bx2, outv,
     in_sem, w_sem, out_sem, a_send, a_recv, g_send, g_recv, r_send, r_recv,
 ):
     slots = outer * inner * CAP
@@ -148,17 +148,18 @@
                 block, dn[:, rows_of(owner, width)], NT, preferred_element_type=F32
             )
 
-    def gather_step(t, s):
+    def gather_step(s):
         for c in range(chunks):
+            for t in range(2):
+                for d in range(2):
+                    if s < hops(t, d):
+                        gather_copy(t, d, s, c).wait_recv()
+                        if s + 1 < hops(t, d):
+                            gather_copy(t, d, s + 1, c).start()
+        for t in range(2):
             for d in range(2):
                 if s < hops(t, d):
-                    gather_copy(t, d, s, c).wait_recv()
-                    if s + 1 < hops(t, d):
-                        gather_copy(t, d, s + 1, c).start()
-        for d in range(2):
-            if s < hops(t, d):
-                use_block(t, lax.rem(me + (ring - 1 - s if d == 0 else 1 + s), ring))
-                gather_sent(t, d, s)
+                    use_block(t, lax.rem(me + (ring - 1 - s if d == 0 else 1 + s), ring))
 
     def term(u, dest):
         if u == 0:
@@ -173,19 +174,24 @@
             device_id=right if d == 0 else left, device_id_type=MESH,
         )
 
-    def sum_step(u, s):
-        live = [d for d in range(2) if s < hops(u, d)]
-        terms = {}
-        for d in live:
+    def sum_step(s):
+        live = [(u, d) for u in range(2) for d in range(2) if s < hops(u, d)]
+        for u, d in live:
             far = hops(u, d) - s
-            terms[d] = term(u, lax.rem(me + (far if d == 0 else ring - far), ring))
+            value = term(u, lax.rem(me + (far if d == 0 else ring - far), ring))
+            if s > 0:
+                terms[u, d] = value
+                continue
+            sbuf[u, d, 0] = value.astype(BF16)
+            for c in range(chunks):
+                sum_copy(u, d, 0, c).start()
+        if s == 0:
+            return
         for c in range(chunks):
             chunk = pl.ds(c * part, part)
-            for d in live:
-                value = terms[d][c * part:(c + 1) * part]
-                if s > 0:
-                    sum_copy(u, d, s - 1, c).wait_recv()
-                    value = value + rbuf[u, d, s - 1, chunk].astype(F32)
+            for u, d in live:
+                sum_copy(u, d, s - 1, c).wait_recv()
+                value = terms[u, d, chunk] + rbuf[u, d, s - 1, chunk].astype(F32)
                 sbuf[u, d, s, chunk] = value.astype(BF16)
                 sum_copy(u, d, s, c).start()
 
@@ -229,41 +235,34 @@
 
     longest = ring // 2
     for s in range(longest):
-        gather_step(0, s)
-    gate = gu_acc[:, :ff]
-    up = gu_acc[:, ff:]
-    sig = jax.nn.sigmoid(gate)
-    hid[...] = (gate * sig * up).astype(BF16)
-    sum_step(0, 0)
-    for s in range(longest):
-        gather_step(1, s)
+        gather_step(s)
     gate = gu_acc[:, :ff]
     up = gu_acc[:, ff:]
     sig = jax.nn.sigmoid(gate)
     back = back_acc[...]
+    hid[...] = (gate * sig * up).astype(BF16)
     dgu[:, :ff] = (back * up * sig * (1.0 + gate * (1.0 - sig))).astype(BF16)
     dgu[:, ff:] = (back * gate * sig).astype(BF16)
-    sum_step(1, 0)
-    for s in range(1, longest):
-        sum_step(0, s)
-    sum_end(0)
-    for s in range(1, longest):
-        sum_step(1, s)
-        if s == longest // 3:
-            back_turn(0)
-        if s == 2 * longest // 3:
-            back_end(0)
-    sum_end(1)
+    for s in range(longest):
+        sum_step(s)
+    for t in range(2):
+        for d in range(2):
+            for s in range(hops(t, d)):
+                gather_sent(t, d, s)
+    for u in range(2):
+        sum_end(u)
     for u in range(2):
         for d in range(2):
             for s in range(hops(u, d)):
                 sum_sent(u, d, s)
-        swap_wait(2, 0, bk1.at[0], bx1.at[0], False, True) if u == 0 else None
-    back_turn(1)
-    swap_wait(3, 0, bk2.at[0], bx2.at[0], True, True)
-    swap_wait(2, 1, bk1.at[1], bx1.at[1], False, True)
-    back_end(1)
-    swap_wait(3, 1, bk2.at[1], bx2.at[1], True, True)
+    for u in range(2):
+        back_turn(u)
+    for u in range(2):
+        swap_wait(2, u, bk1.at[u], bx1.at[u], False, True)
+    for u in range(2):
+        back_end(u)
+    for u in range(2):
+        swap_wait(3, u, bk2.at[u], bx2.at[u], True, True)
     for u in range(2):
         pltpu.make_async_copy(outv.at[u], (mixed_ref, gtok_ref)[u], out_sem.at[u]).wait()
 
@@ -276,7 +275,7 @@
     d_model, ff = gate_weight.shape[1:]
     longest = ring // 2
     out = jax.ShapeDtypeStruct((group, width), BF16)
-    any_spec = pl.BlockSpec(memory_space=pl.ANY)
+    any_spec = pl.BlockSpec(memory_space=pltpu.HBM)
     block = (slots, width)
     dma = pltpu.SemaphoreType.DMA
     return pl.pallas_call(
@@ -297,6 +296,7 @@
             pltpu.VMEM((slots, ff), F32),
             pltpu.VMEM((slots, ff), BF16),
             pltpu.VMEM((slots, 2 * ff), BF16),
+            pltpu.VMEM((2, 2) + block, F32),
             pltpu.VMEM((2, 2, longest) + block, BF16),
             pltpu.VMEM((2, 2, longest) + block, BF16),
             pltpu.VMEM((2,) + block, BF16),

time: 151 us -> 111 us (0.74)
  Pallas kernels: 143 us -> 103 us
    pallas_call x1, Pallas kernels: 143 us -> 103 us  [per_device(): pl.pallas_call(functools.partial(kernel, outer, inner, ring, CHUNKS), out...]
where the time goes in v2:
time: 111 us
  Pallas kernels  103 us (93%)
  local copies, waits for them, and re-layouts  7.07 us (6%)
    pallas_call x1, Pallas kernels, per_device(): pl.pallas_call(functools.partial(kernel, outer, inner, ring, CHUNKS), out...  103 us
    unnamed x14, local copies, waits for them, and re-layouts  7.07 us

profile of v2, /device:TPU:1, one launch (start us, length us, event | category | flops | bytes accessed | tf_op | source)
XLA Modules:
  0.0 110.6 jit_solution(10906567987871478806)
XLA Ops:
  0.6 0.0 copy-start.5
  0.6 0.6 copy-done.5
  1.3 0.0 copy-start
  1.3 1.2 %copy-done = bf16[1,4096,128]{2,1,0:T(8,128)(2,1)S(1)} copy-done((bf16[1,4096,128]{2,1,0:T(8,128)(2,1)S(1)}, bf16[1,4096,128]{2,1,0:T(8,128)(2,1)}, u32[]{:S(2)}) %copy-start) | copy-done | bytes 1048600
  2.5 0.0 copy-start.1
  2.5 1.2 %copy-done.1 = bf16[1,4096,128]{2,1,0:T(8,128)(2,1)S(1)} copy-done((bf16[1,4096,128]{2,1,0:T(8,128)(2,1)S(1)}, bf16[1,4096,128]{2,1,0:T(8,128)(2,1)}, u32[]{:S(2)}) %copy-start.1) | copy-done | bytes 1048600
  3.7 0.0 copy-start.2
  3.7 1.2 %copy-done.2 = bf16[1,128,4096]{2,1,0:T(8,128)(2,1)S(1)} copy-done((bf16[1,128,4096]{2,1,0:T(8,128)(2,1)S(1)}, bf16[1,128,4096]{2,1,0:T(8,128)(2,1)}, u32[]{:S(2)}) %copy-start.2) | copy-done | bytes 1048600
  5.0 0.0 copy-start.3
  5.0 0.8 copy-done.3
  5.7 0.0 copy-start.4
  5.7 0.8 copy-done.4
  6.5 102.8 %shard_map.77 = (bf16[64,256]{1,0:T(8,128)(2,1)S(1)}, bf16[64,256]{1,0:T(8,128)(2,1)S(1)}) custom-call(s32[1,64]{1,0:T(1,128)S(1)} %bitcast.1, bf16[64,256]{1,0:T(8,128)(2,1)S(1)} %copy-done.3, bf16[64,256]{1,0:T(8,128)(2,1)S(1)} %copy-done.4, bf16[1,4096,128]{2,1,0:T(8,128)(2,1)S(1)} %copy-done, bf16[1,4096,128]{2,1,0:T(8,128)(2,1)S(1)} %copy-done.1, ...), custom_call_target="tpu_custom_call" | custom-call | flops 805306368 | bytes 3145728 | tf_op jit(solution)/shard_map/pallas_call | solution.py:281
  109.3 0.6 copy.10
  109.9 0.6 copy.11
Async XLA Ops:
  0.6 0.7 copy-start.5
  1.3 1.2 %copy-start = (bf16[1,4096,128]{2,1,0:T(8,128)(2,1)S(1)}, bf16[1,4096,128]{2,1,0:T(8,128)(2,1)}, u32[]{:S(2)}) copy-start(bf16[1,4096,128]{2,1,0:T(8,128)(2,1)} %gate_ref.1) | copy-start | bytes 3145732
  2.5 1.2 %copy-start.1 = (bf16[1,4096,128]{2,1,0:T(8,128)(2,1)S(1)}, bf16[1,4096,128]{2,1,0:T(8,128)(2,1)}, u32[]{:S(2)}) copy-start(bf16[1,4096,128]{2,1,0:T(8,128)(2,1)} %up_ref.1) | copy-start | bytes 3145732
  3.7 1.2 %copy-start.2 = (bf16[1,128,4096]{2,1,0:T(8,128)(2,1)S(1)}, bf16[1,128,4096]{2,1,0:T(8,128)(2,1)}, u32[]{:S(2)}) copy-start(bf16[1,128,4096]{2,1,0:T(8,128)(2,1)} %down_ref.1) | copy-start | bytes 3145732
  5.0 0.8 copy-start.3
  5.7 0.8 copy-start.4

commit v3 on v2

--- a/solution.py
+++ b/solution.py
@@ -10,6 +10,7 @@
 CAP = 2
 INNER = 8
 CHUNKS = 2
+VMEM_LIMIT = 63 * 1024 * 1024
 MESH = pl.DeviceIdType.MESH
 F32 = jnp.float32
 BF16 = jnp.bfloat16
@@ -245,10 +246,10 @@
     dgu[:, ff:] = (back * gate * sig).astype(BF16)
     for s in range(longest):
         sum_step(s)
-    for t in range(2):
-        for d in range(2):
-            for s in range(hops(t, d)):
-                gather_sent(t, d, s)
+        if s < 2:
+            for d in range(2):
+                for sent in range(hops(s, d)):
+                    gather_sent(s, d, sent)
     for u in range(2):
         sum_end(u)
     for u in range(2):
@@ -315,7 +316,7 @@
             dma((2, 2, longest, CHUNKS)),
         ],
         compiler_params=pltpu.CompilerParams(
-            collective_id=0, has_side_effects=True, vmem_limit_bytes=40 * 1024 * 1024
+            collective_id=0, has_side_effects=True, vmem_limit_bytes=VMEM_LIMIT
         ),
         cost_estimate=pl.CostEstimate(
             flops=12 * slots * d_model * ff, bytes_accessed=6 * d_model * ff, transcendentals=slots * ff

time: 111 us -> 106 us (0.955)
  local copies, waits for them, and re-layouts: 7.07 us -> 2 us
    unnamed x14 -> x4, local copies, waits for them, and re-layouts: 7.07 us -> 2 us
where the time goes in v3:
time: 106 us
  Pallas kernels  103 us (97%)
  local copies, waits for them, and re-layouts  2 us (2%)
    pallas_call x1, Pallas kernels, per_device(): pl.pallas_call(functools.partial(kernel, outer, inner, ring, CHUNKS), out...  103 us

profile of v3, /device:TPU:1, one launch (start us, length us, event | category | flops | bytes accessed | tf_op | source)
XLA Modules:
  0.0 105.8 jit_solution(10404668298069739195)
XLA Ops:
  0.6 103.2 %shard_map.77 = (bf16[64,256]{1,0:T(8,128)(2,1)}, bf16[64,256]{1,0:T(8,128)(2,1)}) custom-call(s32[1,64]{1,0:T(1,128)} %bitcast.1, bf16[64,256]{1,0:T(8,128)(2,1)} %tok_ref.1, bf16[64,256]{1,0:T(8,128)(2,1)} %cot_ref.1, bf16[1,4096,128]{2,1,0:T(8,128)(2,1)} %gate_ref.1, bf16[1,4096,128]{2,1,0:T(8,128)(2,1)} %up_ref.1, bf16[1,128,4096]{2,1,0:T(8,128)(2,1)} %down_ref.1), custom_call_target="tpu_custom_call" | custom-call | flops 805306368 | bytes 3145728 | tf_op jit(solution)/shard_map/pallas_call | solution.py:282
  103.8 0.0 copy-start
  103.8 1.4 %copy.10 = bf16[64,256]{1,0:T(8,128)(2,1)} copy(bf16[64,256]{1,0:T(8,128)(2,1)} %get-tuple-element.4) | data formatting | bytes 65536
  105.2 0.0 copy-done
  105.2 0.6 copy.11
Async XLA Ops:
  103.8 1.4 %copy-start = (bf16[64,256]{1,0:T(8,128)(2,1)S(1)}, bf16[64,256]{1,0:T(8,128)(2,1)}, u32[]{:S(2)}) copy-start(bf16[64,256]{1,0:T(8,128)(2,1)} %get-tuple-element.5) | copy-start | bytes 98308
